TPU v7x, 32 devices: a whole 2x2x4 slice. The times are simulated.
32 devices in a mesh: dp: 8 (over z, y), section: 4 (over x, core).
Axes of the slice: x: 2, y: 2, z: 4, core: 2. Of those that a mesh axis runs over, the one named last changes fastest.
Arguments:
- block_input: float32 [4, 8, 256, 512], P(None, 'dp'), may hold values from -20 to 20
- cotangent: float32 [4, 8, 256, 512], P(None, 'dp'), may hold values from -20 to 20
- section_weight: float32 [4, 512, 1024], P('section'), may hold values from -0.25 to 0.25
- section_vectors: float32 [8, 512], P('section'), may hold values from -6 to 1
- norm_params: float32 [4, 512], replicated, may hold values from 0.5 to 1.5
- running_stats: float32 [4, 512], replicated, may hold values from 0.5 to 2
- resets: int32 [4, 8, 4], P(None, 'dp'), may hold values from 1 to 255
- lengths: int32 [4, 8], P(None, 'dp'), may hold values from 128 to 256
Outputs:
- block_output: float32 [4, 8, 256, 512], P('section', 'dp')
- input_grad: float32 [4, 8, 256, 512], P('section', 'dp')
- section_weight_grad: float32 [4, 512, 1024], P('section')
- section_vectors_grad: float32 [8, 512], P('section')
- norm_grad: float32 [4, 512], P('section')
- new_running: float32 [4, 512], P('section')
All inputs are finite; a program needn't handle non-finite values.
Results may differ from a plain program's by a relative error of at most 0.0003.
Values sent between devices are 32-bit elements; how exact they have to be, the bound alone decides.
A program may use at most 192 MiB of HBM per device.

v0:
```python
import functools

import jax
import jax.numpy as jnp
from jax import lax
from jax.experimental import pallas as pl
from jax.experimental.pallas import tpu as pltpu
from jax.sharding import PartitionSpec as P

epsilon = 1e-05
momentum = 0.1
MESH = pl.DeviceIdType.MESH
f32 = jnp.float32
bf16 = jnp.bfloat16
ROWS = 16
UNIT = 256
BAND = 64
CHUNKS = 4
SEGMENTS = (
    ("glu1", 1.8), ("c1", 0.9), ("b1", 0.9), ("stream1", 1.5), ("gate0", 0.8), ("glu0", 1.8),
    ("mixed0", 2.0), ("states0", 0.6), ("c0", 0.9), ("scan0", 2.0), ("b0", 0.9), ("normed0", 1.5),
    ("stream0", 2.5),
)
MAKES = {
    "glu1": (1, 1, (0, 1, 2, 3)), "c1": (1, 0, (0, 1)), "b1": (1, 0, (2, 3)),
    "glu0": (0, 1, (0, 1, 2, 3)), "c0": (0, 0, (0, 1)), "b0": (0, 0, (2, 3)),
}


def far_first(layer, core, j):
    return layer != core


def turned(layer, core, j):
    return 0


def step_kinds(layer, core, j, k, owner):
    halving = [("halve", stage) for stage in range(k)]
    doubling = [("double", stage) for stage in reversed(range(k))]
    if far_first(layer, core, j):
        return [("core", 0)] + ([("far", 0)] + halving + doubling if owner else [])
    return [("core", 0)] + halving + ([("far", k)] + doubling if owner else [])


def planned(k):
    chunk, hop, work = 5.2, 1.5, 0.2
    roles = [(x, core) for x in range(2) for core in range(2)]
    links = {}
    ready = {role: {} for role in roles}
    order = {role: {name: [] for name, _ in SEGMENTS} | {"rest": []} for role in roles}
    now = dict.fromkeys(roles, 0.0)
    place = dict.fromkeys(roles, 0)
    early = {}

    def send(start, names, lasts):
        begin = max([start] + [links.get(name, 0.0) for name in names])
        for name in names:
            links[name] = begin + lasts
        return begin + lasts + hop

    def kinds(role, layer, j):
        return step_kinds(layer, role[1], j, k, role[0] == layer)

    def launch(role, layer, j, kind, stage, at):
        x, core = role
        if kind == "far":
            if x != layer:
                early[(1 - x, core), layer, j] = send(at, [("x", x)], chunk / (1 << stage))
            return
        bit = (stage + turned(layer, core, j)) % k
        lasts = chunk / (2 << stage)
        names = [(x, "z"), (x, "middle"), (x, "middle")] if bit == 2 and k == 3 else [(x, "z" if bit == 1 else bit)]
        for name in names[2:]:
            links[name] = links.get(name, 0.0) + lasts
        ready[role][layer, j] = (kinds(role, layer, j).index((kind, stage)), send(at, names[:2], lasts))

    def run(role, layer, j):
        step, at = ready[role].pop((layer, j))
        now[role] = max(now[role], at) + work
        place_in = SEGMENTS[place[role]][0] if place[role] < len(SEGMENTS) else "rest"
        order[role][place_in].append((layer, j, step))
        whole = step_kinds(layer, role[1], j, k, True)
        if step + 1 < len(whole):
            kind, stage = whole[step + 1]
            if kind == "far" and role[0] == layer:
                if (role, layer, j) in early:
                    ready[role][layer, j] = (step + 1, early[role, layer, j])
                else:
                    ready[role][layer, j] = (step + 1, None)
            elif kind == "far" or step + 1 < len(kinds(role, layer, j)):
                launch(role, layer, j, kind, stage, now[role])

    while True:
        for role in roles:
            for key, (step, at) in ready[role].items():
                if at is None and (role, *key) in early:
                    ready[role][key] = (step, early[(role, *key)])
        options = []
        for role in roles:
            working = place[role] < len(SEGMENTS)
            known = [
                (at + (3.0 if working and step > 0 else 0.0), key)
                for key, (step, at) in ready[role].items() if at is not None
            ]
            due = [(-key[0], at, key) for at, key in known if at <= now[role]]
            if due:
                options.append((now[role], role, min(due)[2]))
            elif working:
                options.append((now[role], role, None))
            elif known:
                options.append((min(known)[0], role, min(known)[1]))
        if not options:
            break
        _, role, key = min(options, key=lambda option: option[:2])
        if key is not None:
            run(role, *key)
            continue
        name, lasts = SEGMENTS[place[role]]
        place[role] += 1
        now[role] += lasts
        if name in MAKES and MAKES[name][1] != role[1]:
            layer, core, chunks = MAKES[name]
            for j in chunks:
                ready[role[0], core][layer, j] = (0, send(now[role], [("core", role)], chunk / 6))
    return order, now


def split(value):
    high = value.astype(bf16)
    return high, (value - high.astype(f32)).astype(bf16)


def fold(value):
    rows, columns = value.shape
    return jnp.sum(value.reshape(rows // 8, 8, columns), axis=0)


def kernel(n, T, D, *refs):
    (
        block_input, cotangent, matrix_in, vectors_in, norm_in, running_in, resets, lengths,
        out_ref, grad_ref, matrix_out, vector_out, norm_out, running_out,
        xs, g, W, wh, wl, nf, nh, nl, dr, sf, sh, sl, mx, dge, ah, al, jv, js, djh, djl,
        dmx, dmh, dml, dst, ddh, ddl, dn, G, SB, RB, R, V, tab, pw, masks, keep_lane, rowbuf,
        smsg, sbuf, tmp8, vmsg, vbuf, emsg, ebuf,
        XB, nth, ntl, sth, stl, ath, atl, af, coef, lams, gx, lsem, ws, wr, sibs, sibr, rss, rsr, ags, agr, sts, stq, secs, secr, vs, vr,
    ) = refs
    S = D // 2
    k = n.bit_length() - 1
    lanes = D // 128
    d = lax.axis_index("dp")
    s = lax.axis_index("section")
    x, c = s // 2, s % 2
    h = d % 2
    sibling = (d, 2 * x + (1 - c))
    far = (d, 2 * (1 - x) + c)
    pair = (d + 1 - 2 * h, s)

    def remote(src, dst, send, recv, device):
        return pltpu.make_async_remote_copy(
            src_ref=src, dst_ref=dst, send_sem=send, recv_sem=recv, device_id=device,
            device_id_type=MESH,
        )

    W2 = D // 2

    def rows_loop(body, init=None, step=ROWS, total=T, unroll=2):
        def wrapped(i, carry):
            result = body(pl.ds(pl.multiple_of(i * step, step), step), carry)
            return carry if result is None else result

        return lax.fori_loop(0, total // step, wrapped, 0 if init is None else init, unroll=unroll)

    load_x = pltpu.make_async_copy(block_input.at[s, 0], xs.at[0], lsem.at[0])
    load_g = pltpu.make_async_copy(cotangent.at[s, 0], g, lsem.at[1])
    load_w = [
        pltpu.make_async_copy(matrix_in.at[0, :, pl.ds(p * W2, W2)], W.at[s, p], lsem.at[2 + p])
        for p in range(CHUNKS)
    ]
    for copy in load_w:
        copy.start()
    load_x.start()
    load_g.start()

    barrier = pltpu.get_barrier_semaphore()

    def greet(j, carry):
        pl.semaphore_signal(
            barrier, inc=1, device_id=(lax.rem(d + j, n), s), device_id_type=MESH
        )
        return carry

    lax.fori_loop(1, n, greet, 0)
    for j in range(1, 4):
        pl.semaphore_signal(
            barrier, inc=1, device_id=(d, lax.rem(s + j, 4)), device_id_type=MESH
        )
    V[s] = vectors_in[...]

    length = lengths[0, s]
    marks = [resets[s, 0, i] for i in range(resets.shape[2])]
    token = lax.broadcasted_iota(jnp.int32, (T, 128), 0)
    place = token % 8

    def free(low, high):
        hit = None
        for mark in marks:
            inside = (mark >= low) & (mark <= high)
            hit = inside if hit is None else hit | inside
        return jnp.where(hit, 0.0, 1.0)

    for index, shift in enumerate((1, 2, 4)):
        masks[index] = jnp.where(place >= shift, free(token - shift + 1, token), 0.0)
        masks[4 + index] = jnp.where(place + shift <= 7, free(token + 1, token + shift), 0.0)
    masks[3] = free(token - place, token)
    masks[7] = free(token + 1, token - place + 8)
    keep_lane[...] = jnp.where(token > 0, free(token, token), 0.0)

    def usable_at(rows):
        spot = lax.broadcasted_iota(jnp.int32, (ROWS, 128), 0) + rows.start
        mask = jnp.where(spot < length, 1.0, 0.0).astype(f32)
        return jnp.concatenate([mask] * lanes, axis=1)

    def halves(mask):
        return jnp.concatenate([mask] * (S // 128), axis=1)

    count = jnp.full((1, D), length.astype(f32), f32)

    def send_round(index, tiles):
        def go(j, carry):
            remote(
                smsg.at[index, pl.ds(0, tiles)], sbuf.at[index, d, pl.ds(0, tiles)],
                sts.at[index, j], stq.at[index, j], (lax.rem(d + j, n), s),
            ).start()
            return carry

        lax.fori_loop(1, n, go, 0)

    def wait_round(index, tiles):
        def go(j, carry):
            remote(
                smsg.at[index, pl.ds(0, tiles)], sbuf.at[index, d, pl.ds(0, tiles)],
                sts.at[index, j], stq.at[index, j], (lax.rem(d + j, n), s),
            ).wait()
            return carry

        lax.fori_loop(1, n, go, 0)

    def pack(index, tile, first, second):
        for j in range(lanes):
            smsg[index, tile, j : j + 1, :] = first[:, 128 * j : 128 * j + 128]
            smsg[index, tile, lanes + j : lanes + j + 1, :] = second[:, 128 * j : 128 * j + 128]

    def unpack(value):
        tmp8[...] = value
        row = [tmp8[j : j + 1, :] for j in range(2 * lanes)]
        return jnp.concatenate(row[:lanes], axis=1), jnp.concatenate(row[lanes:], axis=1)

    def local_moments(layer):
        def first(rows, total):
            return total + fold(usable_at(rows) * xs[layer, rows, :])

        total = jnp.sum(rows_loop(first, jnp.zeros((8, D), f32)), axis=0, keepdims=True)
        mean = total / jnp.maximum(count, 1.0)

        def second(rows, squares):
            shifted = xs[layer, rows, :] - mean
            return squares + fold(usable_at(rows) * shifted * shifted)

        squares = jnp.sum(rows_loop(second, jnp.zeros((8, D), f32)), axis=0, keepdims=True)
        pack(layer, 0, total, squares)
        if layer == 0:
            smsg[0, 1] = jnp.full((8, 128), length.astype(f32), f32)

    def join_moments(layer):
        sbuf[layer, d, 0] = smsg[layer, 0]
        if layer == 0:
            sbuf[0, d, 1] = smsg[0, 1]

        def add(j, carry):
            return carry[0] + sbuf[layer, j, 0], carry[1] + sbuf[0, j, 1]

        zero = jnp.zeros((8, 128), f32)
        total, counted = lax.fori_loop(0, n, add, (zero, zero))
        tmp8[...] = total / counted
        center = tmp8[0:lanes, :]

        def between(j, carry):
            there = sbuf[0, j, 1][0:lanes, :]
            apart = sbuf[layer, j, 0][0:lanes, :] / jnp.maximum(there, 1.0) - center
            return carry + there * apart * apart

        apart = lax.fori_loop(0, n, between, jnp.zeros((lanes, 128), f32))
        center_row, spread_row = unpack(total / counted)
        tmp8[0:lanes, :] = apart / counted[0:lanes, :]
        apart_row = jnp.concatenate([tmp8[j : j + 1, :] for j in range(lanes)], axis=1)
        count_row = jnp.concatenate([counted[0:1, :]] * lanes, axis=1)
        return center_row, spread_row + apart_row, count_row

    quarter = D // 4

    def rows_of(q, p, half, core):
        start = pl.multiple_of((2 * half + core) * quarter, quarter)
        return W.at[q, p, pl.ds(start, quarter)]

    def own_copy(p):
        return remote(W.at[s, p], W.at[s, p], ws.at[0, p], wr.at[0, p], sibling)

    def far_copy_of(i):
        ref = rows_of(2 * x + i // CHUNKS, i % CHUNKS, h, c)
        return remote(ref, ref, ws.at[1, i], wr.at[1, i], far)

    def hand_copy(kind, i):
        half = 1 - h if kind == 4 else h
        ref = rows_of(2 * (1 - x) + i // CHUNKS, i % CHUNKS, half, c)
        return remote(ref, ref, ws.at[kind, i], wr.at[kind, i], pair if kind == 3 else sibling)

    def convert(q, p):
        def body(rows, carry):
            high, low = split(W[q, p, rows, :])
            wh[q, rows, p * W2 : p * W2 + W2] = high
            wl[q, rows, p * W2 : p * W2 + W2] = low

        rows_loop(body, total=D, unroll=4)

    def arrive(i):
        far_copy_of(i).wait_recv()
        hand_copy(2, i).start()
        hand_copy(3, i).start()

    def arrive_pair(i):
        hand_copy(3, i).wait_recv()
        hand_copy(4, i).start()

    def arrive_sibling(i):
        hand_copy(2, i).wait_recv()
        hand_copy(4, i).wait_recv()

    def send_far(i):
        far_copy_of(i).start()

    def convert_own():
        for q in range(2):
            for p in range(CHUNKS):
                convert(2 * x + q, p)

    def convert_far(plane, q, p):
        @pl.when(x == plane)
        def _():
            convert(q, p)

    events = []
    for i in range(2 * CHUNKS + 2):
        if i < 2 * CHUNKS:
            events.append((arrive, i))
        if 0 <= i - 1 < 2 * CHUNKS:
            events.append((arrive_pair, i - 1))
        if 0 <= i - 2 < 2 * CHUNKS:
            events.append((arrive_sibling, i - 2))
    passed = [0, 0]

    def until(plane, what):
        stop = events.index(what) + 1 if what is not None else len(events)
        todo = events[passed[plane] : stop]
        passed[plane] = max(passed[plane], stop)
        if todo:

            @pl.when(x == plane)
            def _():
                for event, i in todo:
                    event(i)

    def vector_copy(j):
        return remote(V.at[s], V.at[s], vs.at[j], vr.at[j], (d, lax.rem(s + j, 4)))

    def bit_value(task, stage):
        return 1 << ((stage + turned(*task)) % k)

    def my_bit(task, stage):
        return (d // bit_value(task, stage)) % 2

    def partner(task, stage):
        return (d + bit_value(task, stage) * (1 - 2 * my_bit(task, stage)), s)

    def segment(task, stage, mine):
        start = 0
        for earlier in range(stage):
            start = start + my_bit(task, earlier) * (D >> (earlier + 1))
        bit = my_bit(task, stage) if mine else 1 - my_bit(task, stage)
        size = D >> (stage + 1)
        return pl.ds(pl.multiple_of(start + bit * size, size), size)

    def landing(stage):
        size = D >> (stage + 1) if stage < k else D >> k
        return pl.ds(D - (D >> stage), size)

    def column(core, j):
        return j if core == 1 else (j + 2) % CHUNKS

    def sibling_copy(core, layer, j):
        return remote(
            G.at[2 * layer + 1 - core, column(1 - core, j)], SB.at[layer, j],
            sibs.at[layer, j], sibr.at[layer, j], sibling,
        )

    def mine_of(task):
        layer, core, j = task
        return G.at[2 * layer + core, column(core, j)]

    def halving_copy(task, stage):
        layer, core, j = task
        return remote(
            mine_of(task).at[segment(task, stage, False)], RB.at[layer, j, landing(stage)],
            rss.at[layer, j, stage], rsr.at[layer, j, stage], partner(task, stage),
        )

    def far_copy(task):
        layer, core, j = task
        if far_first(*task):
            source, target = mine_of(task), XB.at[j]
        else:
            source, target = mine_of(task).at[segment(task, k - 1, True)], RB.at[layer, j, landing(k)]
        return remote(source, target, rss.at[layer, j, k], rsr.at[layer, j, k], far)

    def doubling_copy(task, stage):
        layer, core, j = task
        ref = R.at[column(core, j), segment(task, stage, True)]
        return remote(ref, ref, ags.at[j, stage], agr.at[j, stage], partner(task, stage))

    def result_copy(j):
        return pltpu.make_async_copy(R.at[j], matrix_out.at[0, :, pl.ds(j * W2, W2)], lsem.at[6 + j])

    def add_rows(target, start, mine, mine_start, source, source_start, size):
        step = min(size, 32)

        def body(i, carry):
            a, b, e = (
                pl.ds(pl.multiple_of(first + i * step, 8), step)
                for first in (start, mine_start, source_start)
            )
            target[a, :] = mine[b, :] + source[e, :]
            return carry

        lax.fori_loop(0, size // step, body, 0, unroll=min(2, size // step))

    def advance(role, layer, j, step):
        plane, core = role
        task = (layer, core, j)
        whole = step_kinds(layer, core, j, k, True)
        kind, stage = whole[step]
        after = whole[step + 1] if step + 1 < len(whole) else None
        mine, total = mine_of(task), R.at[column(core, j)]
        target = total if after is not None and after[0] == "double" else mine
        if kind == "core":
            sibling_copy(core, layer, j).wait_recv()
            add_rows(target, 0, mine, 0, SB.at[layer, j], 0, D)
        elif kind == "far":
            far_copy(task).wait_recv()
            if far_first(*task):
                add_rows(target, 0, mine, 0, XB.at[j], 0, D)
            else:
                kept = segment(task, k - 1, True)
                add_rows(target, kept.start, mine, kept.start, RB.at[layer, j], landing(k).start, kept.size)
        elif kind == "halve":
            halving_copy(task, stage).wait()
            kept = segment(task, stage, True)
            add_rows(target, kept.start, mine, kept.start, RB.at[layer, j], landing(stage).start, kept.size)
        else:
            doubling_copy(task, stage).wait()
        if after is None:
            result_copy(column(core, j)).start()
        elif after[0] == "far":
            if plane != layer:
                far_copy(task).start()
        elif after[0] == "halve":
            halving_copy(task, after[1]).start()
        else:
            doubling_copy(task, after[1]).start()

    plans = planned(k)[0]

    def by_role(work):
        for role in plans:
            todo = work(role)
            if todo:

                @pl.when(s == 2 * role[0] + role[1])
                def _():
                    for layer, j, step in todo:
                        advance(role, layer, j, step)

    def steps_before(name):
        by_role(lambda role: plans[role][name])

    load_x.wait()
    local_moments(0)
    pl.semaphore_wait(barrier, n - 1 + 3)
    send_round(0, 2)
    for j in range(1, 4):
        vector_copy(j).start()
    for p in range(CHUNKS):
        load_w[p].wait()

        @pl.when(c == 0)
        def _():
            send_far(p)

        own_copy(p).start()
    for p in range(CHUNKS):
        own_copy(p).wait_recv()

        @pl.when(c == 1)
        def _():
            send_far(p)

    for p in range(CHUNKS):
        send_far(CHUNKS + p)
    for j in range(1, 4):
        vector_copy(j).wait()

    for layer in range(2):
        rates = V[2 * layer, 1:2, 0:S]
        angles = V[2 * layer, 1:2, S:D]
        grown = jnp.exp(rates)
        radius = jnp.exp(-grown)
        phases = jnp.exp(angles)
        cosine, sine = jnp.cos(phases), jnp.sin(phases)
        scaling = jnp.sqrt(1.0 - radius * radius)
        for index, row in enumerate((grown, radius, phases, cosine, sine, scaling)):
            coef[layer, index : index + 1, :] = row
        power = [(radius * cosine, radius * sine)]
        for _ in range(3):
            a, b = power[-1]
            power.append((a * a - b * b, 2.0 * a * b))
        for index, (a, b) in enumerate(power):
            pw[layer, 2 * index] = jnp.broadcast_to(a, (8, S))
            pw[layer, 2 * index + 1] = jnp.broadcast_to(b, (8, S))
        pw[layer, 8] = jnp.broadcast_to(scaling, (8, S))
        row = lax.broadcasted_iota(jnp.int32, (8, S), 0)
        for way, exponent in enumerate((row + 1, 8 - row)):
            a = jnp.ones((8, S), f32)
            b = jnp.zeros((8, S), f32)
            for index in range(4):
                on = (exponent // (1 << index)) % 2 == 1
                pa, pb = pw[layer, 2 * index], pw[layer, 2 * index + 1]
                a, b = jnp.where(on, a * pa - b * pb, a), jnp.where(on, a * pb + b * pa, b)
            tab[layer, 2 * way] = a
            tab[layer, 2 * way + 1] = b

    def forward_scan(layer):
        scale = pw[layer, 8]
        table_r, table_i = tab[layer, 0], tab[layer, 1]

        def body(i, carry):
            cr, ci = carry
            pieces = []
            for part in range(ROWS // 8):
                rows = pl.ds(pl.multiple_of(i * ROWS + part * 8, 8), 8)
                br = scale * dr[layer, rows, 0:S]
                bi = scale * dr[layer, rows, S:D]
                for index, shift in enumerate((1, 2, 4)):
                    mask = halves(masks[index, rows, :])
                    pr, pi = pw[layer, 2 * index], pw[layer, 2 * index + 1]
                    rr = mask * pltpu.roll(br, shift, 0)
                    ri = mask * pltpu.roll(bi, shift, 0)
                    br, bi = br + (pr * rr - pi * ri), bi + (pr * ri + pi * rr)
                whole = halves(masks[3, rows, :])
                mr, mi = whole * table_r, whole * table_i
                hr = br + (mr * cr - mi * ci)
                hi = bi + (mr * ci + mi * cr)
                er, ei = (jnp.broadcast_to(v[7:8, :], (8, S)) for v in (mr, mi))
                lr, li = (jnp.broadcast_to(v[7:8, :], (8, S)) for v in (br, bi))
                cr, ci = lr + (er * cr - ei * ci), li + (er * ci + ei * cr)
                pieces.append(jnp.concatenate([hr, hi], axis=1))
            both = jnp.concatenate(pieces, axis=0)
            rows = pl.ds(pl.multiple_of(i * ROWS, ROWS), ROWS)
            sf[layer, rows, :] = both
            high, low = split(both)
            sh[rows, :] = high
            sl[rows, :] = low
            return cr, ci

        zero = jnp.zeros((8, S), f32)
        lax.fori_loop(0, T // ROWS, body, (zero, zero), unroll=2)

    def backward_scan(layer):
        scale = pw[layer, 8]
        table_r, table_i = tab[layer, 2], tab[layer, 3]
        top = lax.broadcasted_iota(jnp.int32, (8, S), 0) == 0

        def body(i, carry):
            cr, ci, lam_r, lam_i, gam = carry
            pieces = [None] * (ROWS // 8)
            for part in reversed(range(ROWS // 8)):
                start = T - ROWS - i * ROWS + part * 8
                rows = pl.ds(pl.multiple_of(start, 8), 8)
                before = pl.ds(pl.multiple_of(jnp.maximum(start - 8, 0), 8), 8)
                br = dst[rows, 0:S]
                bi = dst[rows, S:D]
                for index, shift in enumerate((1, 2, 4)):
                    mask = halves(masks[4 + index, rows, :])
                    pr, pi = pw[layer, 2 * index], pw[layer, 2 * index + 1]
                    rr = mask * pltpu.roll(br, 8 - shift, 0)
                    ri = mask * pltpu.roll(bi, 8 - shift, 0)
                    br, bi = br + (pr * rr + pi * ri), bi + (pr * ri - pi * rr)
                whole = halves(masks[7, rows, :])
                mr, mi = whole * table_r, whole * table_i
                gr = br + (mr * cr + mi * ci)
                gi = bi + (mr * ci - mi * cr)
                er, ei = (jnp.broadcast_to(v[0:1, :], (8, S)) for v in (mr, mi))
                lr, li = (jnp.broadcast_to(v[0:1, :], (8, S)) for v in (br, bi))
                cr, ci = lr + (er * cr + ei * ci), li + (er * ci - ei * cr)
                keep = halves(keep_lane[rows, :])
                pr, pi = (
                    keep * jnp.where(
                        top, pltpu.roll(sf[layer, before, cut], 1, 0), pltpu.roll(sf[layer, rows, cut], 1, 0)
                    )
                    for cut in (slice(0, S), slice(S, D))
                )
                lam_r = lam_r + (gr * pr + gi * pi)
                lam_i = lam_i + (gi * pr - gr * pi)
                gam = gam + (gr * dr[layer, rows, 0:S] + gi * dr[layer, rows, S:D])
                pieces[part] = jnp.concatenate([scale * gr, scale * gi], axis=1)
            rows = pl.ds(pl.multiple_of(T - ROWS - i * ROWS, ROWS), ROWS)
            high, low = split(jnp.concatenate(pieces, axis=0))
            ddh[rows, :] = high
            ddl[rows, :] = low
            return cr, ci, lam_r, lam_i, gam

        zero = jnp.zeros((8, S), f32)
        _, _, lam_r, lam_i, gam = lax.fori_loop(
            0, T // ROWS, body, (zero,) * 5, unroll=2
        )
        for index, value in enumerate((lam_r, lam_i, gam)):
            lams[layer, index] = value

    def decay_back(layer):
        lam_r, lam_i, gam = (jnp.sum(lams[layer, index], axis=0, keepdims=True) for index in range(3))
        grown, radius, phases, cosine, sine, scaling = (
            coef[layer, index : index + 1, :] for index in range(6)
        )
        along = lam_r * cosine + lam_i * sine
        across = lam_i * cosine - lam_r * sine
        da = along - gam * radius / scaling
        vmsg[4 * layer + 1 : 4 * layer + 2, 0:S] = -radius * grown * da
        vmsg[4 * layer + 1 : 4 * layer + 2, S:D] = radius * phases * across

    tiles = [slice(i, i + D // 2) for i in range(0, D, D // 2)]

    def tile(index, start=0):
        return slice(start + index * UNIT, start + (index + 1) * UNIT)

    def multiply(left, right, depth, columns, keep, transpose=False):
        left_high, left_low = left
        parts = left_high.shape[0] // BAND
        pairs = columns // 2

        def run(*sums):
            def sum_of(pair, unit, part):
                return sums[((pair % 2) * 2 + unit) * parts + part]

            def pop(pair):
                for part in range(parts):
                    for unit in range(2):
                        keep(
                            2 * pair + unit, slice(part * BAND, part * BAND + BAND),
                            pltpu.matmul_pop(sum_of(pair, unit, part)),
                        )

            sequence = [
                (pair, step, low)
                for pair in range(pairs) for step in range(depth // UNIT) for low in range(2)
            ]

            def push(index):
                pair, step, low = sequence[index]
                for unit in range(2):
                    pltpu.matmul_push_rhs(
                        right(low, step, 2 * pair + unit), index % 2, unit, transpose=transpose
                    )

            push(0)
            for index, (pair, step, low) in enumerate(sequence):
                for turn, source in enumerate((left_high,) if low else (left_high, left_low)):
                    for part in range(parts):
                        first = turn == 0 and part == 0
                        rows = source[part * BAND : part * BAND + BAND, tile(step)]
                        for unit in range(2):
                            pltpu.matmul_acc_lhs(
                                sum_of(pair, unit, part), rows,
                                load_staged_rhs=index % 2 if first else None,
                            )
                        if first and index + 1 < len(sequence):
                            push(index + 1)
                if pair > 0 and step == 0 and low == 0:
                    pop(pair - 1)
            pop(pairs - 1)

        pl.run_scoped(
            run,
            *[pltpu.ACC(unit)((BAND, UNIT), f32) for _ in range(2) for unit in range(2) for _ in range(parts)],
        )

    def weight_tiles(q, start=0):
        return lambda part, step, column: (wh, wl)[part][q, tile(step), tile(column, start)]

    def weight_tiles_across(q, start=0):
        return lambda part, step, column: (wh, wl)[part][q, tile(column), tile(step, start)]

    def keep_in(ref):
        def keep(column, rows, value):
            ref[rows, tile(column)] = value

        return keep

    def forward(layer, center, inverse):
        gain = norm_in[2 * layer : 2 * layer + 1, :]
        offset = norm_in[2 * layer + 1 : 2 * layer + 2, :]
        skip = V[2 * layer, 0:1, :]
        mixer, glu = 2 * layer, 2 * layer + 1
        away = 1 - layer

        def normalise(rows, carry):
            normed = gain * ((xs[layer, rows, :] - center) * inverse) + offset
            nf[layer, rows, :] = normed
            high, low = split(normed)
            nh[rows, :] = high
            nl[rows, :] = low

        rows_loop(normalise)
        until(away, (arrive_sibling, 1))
        for p in range(2):
            convert_far(away, mixer, p)
        multiply((nh, nl), weight_tiles(mixer), D, D // UNIT, keep_in(dr.at[layer]))
        if layer == 0:
            until(0, (arrive, 1))
        forward_scan(layer)
        until(away, (arrive_sibling, 3))
        for p in range(2, 4):
            convert_far(away, mixer, p)
        multiply((sh, sl), weight_tiles(mixer, D), D, D // UNIT, keep_in(mx))
        until(away, (arrive, 5))
        if layer == 0:
            until(0, (arrive_pair, 1))

        def activate(rows, carry):
            mixed = mx[rows, :] + skip * nf[layer, rows, :]
            phi = 0.5 * (1.0 + lax.erf(mixed * 0.7071067811865476))
            dge[layer, rows, :] = phi + mixed * (0.3989422804014327 * jnp.exp(-0.5 * mixed * mixed))
            active = mixed * phi
            af[rows, :] = active
            high, low = split(active)
            ah[rows, :] = high
            al[rows, :] = low

        rows_loop(activate)
        for p in range(CHUNKS):
            until(away, (arrive_sibling, CHUNKS + p))
            convert_far(away, glu, p)
        multiply((ah, al), weight_tiles(glu), D, D // UNIT, keep_in(jv.at[layer]))
        multiply((ah, al), weight_tiles(glu, D), D, D // UNIT, keep_in(js.at[layer]))
        if layer == 0:
            until(0, (arrive_pair, 2))
        value_bias = V[2 * layer + 1, 0:1, :]
        gate_bias = V[2 * layer + 1, 1:2, :]
        target = xs.at[layer + 1]

        def gate(rows, carry):
            value = jv[layer, rows, :] + value_bias
            sig = 1.0 / (1.0 + jnp.exp(-(js[layer, rows, :] + gate_bias)))
            jv[layer, rows, :] = value
            js[layer, rows, :] = sig
            target[rows, :] = xs[layer, rows, :] + usable_at(rows) * (value * sig)

        rows_loop(gate)

    def gate_back(layer):
        def body(rows, carry):
            dgated = usable_at(rows) * g[rows, :]
            value, sig = jv[layer, rows, :], js[layer, rows, :]
            dvalue = dgated * sig
            dgate = dvalue * value * (1.0 - sig)
            for cut, part in ((slice(0, D), dvalue), (slice(D, 2 * D), dgate)):
                high, low = split(part)
                djh[rows, cut] = high
                djl[rows, cut] = low
            return carry[0] + fold(dvalue), carry[1] + fold(dgate)

        zero = jnp.zeros((8, D), f32)
        first, second = rows_loop(body, (zero, zero))
        vmsg[4 * layer + 2 : 4 * layer + 3, :] = jnp.sum(first, axis=0, keepdims=True)
        vmsg[4 * layer + 3 : 4 * layer + 4, :] = jnp.sum(second, axis=0, keepdims=True)

    def mixed_back(layer):
        glu = 2 * layer + 1
        multiply((djh, djl), weight_tiles_across(glu), 2 * D, D // UNIT, keep_in(dmx), transpose=True)

        def body(rows, skip_sum):
            dmixed = dge[layer, rows, :] * dmx[rows, :]
            dmx[rows, :] = dmixed
            high, low = split(dmixed)
            dmh[rows, :] = high
            dml[rows, :] = low
            return skip_sum + fold(dmixed * nf[layer, rows, :])

        skip_sum = rows_loop(body, jnp.zeros((8, D), f32))
        vmsg[4 * layer : 4 * layer + 1, :] = jnp.sum(skip_sum, axis=0, keepdims=True)

    def states_back(layer):
        multiply(
            (dmh, dml), weight_tiles_across(2 * layer, D), D, D // UNIT, keep_in(dst), transpose=True
        )

    def turn(layer):
        for source, high_ref, low_ref in ((nf.at[layer], nth, ntl), (sf.at[layer], sth, stl), (af, ath, atl)):
            for t in tiles:
                for u in range(0, T, 128):
                    high, low = split(source[u : u + 128, t].T)
                    high_ref[layer, t, u : u + 128] = high
                    low_ref[layer, t, u : u + 128] = low

    def weight_back(q, chunks, left, right, columns):
        def keep(column, rows, value):
            G[q, chunks[column], rows, :] = value

        multiply(
            left, lambda part, step, column: right[part][tile(step), tile(column)], T, columns, keep
        )

    def hand_over(core, layer, chunks):
        @pl.when(c == core)
        def _():
            for j in chunks:
                sibling_copy(core, layer, j).start()

    def glu_back(layer):
        weight_back(
            2 * layer + 1, range(CHUNKS), (ath.at[layer], atl.at[layer]), (djh, djl), CHUNKS
        )
        hand_over(0, layer, range(CHUNKS))

    def c_back(layer):
        weight_back(2 * layer, (2, 3), (sth.at[layer], stl.at[layer]), (dmh, dml), 2)
        hand_over(1, layer, (0, 1))

    def b_back(layer):
        weight_back(2 * layer, (0, 1), (nth.at[layer], ntl.at[layer]), (ddh, ddl), 2)
        hand_over(1, layer, (2, 3))

    def normed_back(layer, center, inverse):
        skip = V[2 * layer, 0:1, :]
        multiply((ddh, ddl), weight_tiles_across(2 * layer), D, D // UNIT, keep_in(dn), transpose=True)

        def body(rows, carry):
            dnormed = skip * dmx[rows, :] + dn[rows, :]
            dn[rows, :] = dnormed
            scaled = (xs[layer, rows, :] - center) * inverse
            return carry[0] + fold(dnormed * scaled), carry[1] + fold(dnormed)

        zero = jnp.zeros((8, D), f32)
        gain_sum, offset_sum = rows_loop(body, (zero, zero))
        pack(
            2 + layer, 0, jnp.sum(gain_sum, axis=0, keepdims=True),
            jnp.sum(offset_sum, axis=0, keepdims=True),
        )
        send_round(2 + layer, 1)

    def stream_back(layer, center, inverse, counted):
        wait_round(2 + layer, 1)
        sbuf[2 + layer, d, 0] = smsg[2 + layer, 0]
        total = lax.fori_loop(
            0, n, lambda j, carry: carry + sbuf[2 + layer, j, 0], jnp.zeros((8, 128), f32)
        )
        gain_total, offset_total = unpack(total)
        emsg[2 * layer, 2:3, :] = gain_total
        emsg[2 * layer + 1, 2:3, :] = offset_total
        factor = norm_in[2 * layer : 2 * layer + 1, :] * inverse
        gain_part, offset_part = gain_total / counted, offset_total / counted
        target = gx if layer == 0 else g

        def body(rows, carry):
            scaled = (xs[layer, rows, :] - center) * inverse
            usable = usable_at(rows)
            target[rows, :] = g[rows, :] + factor * (
                dn[rows, :] - usable * (offset_part + scaled * gain_part)
            )

        rows_loop(body)

    convert_own()
    wait_round(0, 2)
    for layer in range(2):
        if layer == 1:
            local_moments(1)
            send_round(1, 1)
            turn(0)
            until(0, (arrive_sibling, 1))
            wait_round(1, 1)
        center, spread, counted = join_moments(layer)
        emsg[2 * layer, 3:4, :] = center
        emsg[2 * layer + 1, 3:4, :] = spread
        inverse = lax.rsqrt(spread + epsilon)
        rowbuf[2 * layer : 2 * layer + 1, :] = center
        rowbuf[2 * layer + 1 : 2 * layer + 2, :] = inverse
        forward(layer, center, inverse)

    store_out = pltpu.make_async_copy(xs.at[2], out_ref, lsem.at[10])
    store_grad = pltpu.make_async_copy(gx, grad_ref, lsem.at[11])
    store_out.start()

    load_g.wait()
    center, inverse = rowbuf[2:3, :], rowbuf[3:4, :]
    gate_back(1)
    mixed_back(1)
    states_back(1)
    backward_scan(1)
    normed_back(1, center, inverse)
    turn(1)
    glu_back(1)
    steps_before("c1")
    c_back(1)
    steps_before("b1")
    b_back(1)
    steps_before("stream1")
    stream_back(1, center, inverse, counted)

    center, inverse = rowbuf[0:1, :], rowbuf[1:2, :]
    for name, work in (
        ("gate0", lambda: gate_back(0)),
        ("glu0", lambda: glu_back(0)),
        ("mixed0", lambda: mixed_back(0)),
        ("states0", lambda: states_back(0)),
        ("c0", lambda: c_back(0)),
        ("scan0", lambda: backward_scan(0)),
        ("b0", lambda: b_back(0)),
        ("normed0", lambda: normed_back(0, center, inverse)),
        ("stream0", lambda: stream_back(0, center, inverse, counted)),
    ):
        steps_before(name)
        work()

    store_grad.start()

    def vector_round(j):
        return remote(vmsg, vbuf.at[d], sts.at[4, j], stq.at[4, j], (lax.rem(d + j, n), s))

    for layer in range(2):
        decay_back(layer)

    def go(j, carry):
        vector_round(j).start()
        return carry

    def owner_copy(j):
        to = lax.rem(s + j, 4)
        return remote(emsg.at[to], ebuf.at[s], secs.at[j], secr.at[j], (d, to))

    lax.fori_loop(1, n, go, 0)
    def rest(part):
        def of(role):
            steps = plans[role]["rest"]
            cut = len(steps) // 3
            return steps[:cut] if part == 0 else steps[cut:]

        return of

    by_role(rest(0))

    def arrived(j, carry):
        vector_round(j).wait()
        return carry

    lax.fori_loop(1, n, arrived, 0)
    vbuf[d] = vmsg[...]
    total = lax.fori_loop(0, n, lambda j, carry: carry + vbuf[j], jnp.zeros((8, D), f32))
    for q in range(4):
        emsg[q, 0:2, :] = total[2 * q : 2 * q + 2, :]
    for j in range(1, 4):
        owner_copy(j).start()
    by_role(rest(1))

    for j in range(1, 4):
        owner_copy(j).wait()
    ebuf[s] = emsg[s]
    vector_total = jnp.zeros((2, D), f32)
    norm_total = jnp.zeros((1, D), f32)
    current = jnp.zeros((1, D), f32)
    for q in range(4):
        current = jnp.where(s == q, running_in[q : q + 1, :], current)
    for m in range(4):
        vector_total = vector_total + ebuf[m, 0:2, :]
        norm_total = norm_total + ebuf[m, 2:3, :]
        current = (1.0 - momentum) * current + momentum * ebuf[m, 3:4, :]
    vector_out[...] = vector_total
    norm_out[...] = norm_total
    running_out[...] = current

    for p in range(CHUNKS):
        own_copy(p).wait_send()
    for i in range(2 * CHUNKS):
        far_copy_of(i).wait_send()
        for kind in (2, 3, 4):
            hand_copy(kind, i).wait_send()
    for core in range(2):

        @pl.when(c == core)
        def _():
            for layer in range(2):
                for j in range(CHUNKS):
                    sibling_copy(core, layer, j).wait_send()

                    @pl.when(x != layer)
                    def _():
                        far_copy((layer, core, j)).wait_send()


    for j in range(CHUNKS):
        result_copy(j).wait()
    store_out.wait()
    store_grad.wait()


def finish(count, *refs):
    given, results, held, sems = refs[:count], refs[count : 2 * count], refs[2 * count : 3 * count], refs[-1]
    steps = [
        [pltpu.make_async_copy(a, b, sems.at[way, i]) for i, (a, b) in enumerate(zip(*pair))]
        for way, pair in enumerate(((given, held), (held, results)))
    ]
    for copy in steps[0]:
        copy.start()
    for first, second in zip(*steps):
        first.wait()
        second.start()
    for copy in steps[1]:
        copy.wait()


def solution(mesh):
    n = mesh.shape["dp"]
    k = n.bit_length() - 1
    assert mesh.shape["section"] == 4 and n == 1 << k and k >= 1

    def shards(block_input, cotangent, matrix, vectors, norm_params, running, resets, lengths):
        micro, rows, T, D = block_input.shape
        assert micro == 4 and rows == 1
        S = D // 2
        vmem = lambda shape, dtype=f32: pltpu.VMEM(shape, dtype)
        dma = lambda *shape: pltpu.SemaphoreType.DMA(shape)
        scratch = [
            vmem((3, T, D)), vmem((T, D)),
            vmem((4, 4, D, S)), vmem((4, D, 2 * D), bf16), vmem((4, D, 2 * D), bf16),
            vmem((2, T, D)), vmem((T, D), bf16), vmem((T, D), bf16),
            vmem((2, T, D)),
            vmem((2, T, D)), vmem((T, D), bf16), vmem((T, D), bf16),
            vmem((T, D)),
            vmem((2, T, D)),
            vmem((T, D), bf16), vmem((T, D), bf16),
            vmem((2, T, D)), vmem((2, T, D)),
            vmem((T, 2 * D), bf16), vmem((T, 2 * D), bf16),
            vmem((T, D)), vmem((T, D), bf16), vmem((T, D), bf16),
            vmem((T, D)),
            vmem((T, D), bf16), vmem((T, D), bf16),
            vmem((T, D)),
            vmem((4, 4, D, S)), vmem((2, 4, D, S)), vmem((2, 4, D, S)), vmem((4, D, S)),
            vmem((4, 2, D)),
            vmem((2, 4, 8, S)), vmem((2, 9, 8, S)),
            vmem((8, T, 128)), vmem((T, 128)),
            vmem((8, D)),
            vmem((4, 2, 8, 128)), vmem((4, n, 2, 8, 128)), vmem((8, 128)),
            vmem((8, D)), vmem((n, 8, D)), vmem((4, 4, D)), vmem((4, 4, D)),
            vmem((4, D, S)),
            *[vmem((2, D, T), bf16)] * 6,
            vmem((T, D)),
            vmem((2, 8, S)), vmem((2, 3, 8, S)),
            vmem((T, D)),
            dma(12), dma(5, 8), dma(5, 8), dma(2, 4), dma(2, 4),
            dma(2, 4, k + 1), dma(2, 4, k + 1), dma(4, k), dma(4, k),
            dma(5, n), dma(5, n), dma(4), dma(4), dma(4), dma(4),
        ]
        any_space = pl.BlockSpec(memory_space=pl.ANY)
        in_vmem = pl.BlockSpec(memory_space=pltpu.VMEM)
        in_smem = pl.BlockSpec(memory_space=pltpu.SMEM)
        shapes = (
            jax.ShapeDtypeStruct((T, D), f32),
            jax.ShapeDtypeStruct((T, D), f32),
            jax.ShapeDtypeStruct((1, D, 2 * D), f32),
            jax.ShapeDtypeStruct((2, D), f32),
            jax.ShapeDtypeStruct((1, D), f32),
            jax.ShapeDtypeStruct((1, D), f32),
        )
        results = pl.pallas_call(
            functools.partial(kernel, n, T, D),
            out_shape=shapes,
            in_specs=[any_space, any_space, any_space, in_vmem, in_vmem, in_vmem, in_smem, in_smem],
            out_specs=(any_space, any_space, any_space, in_vmem, in_vmem, in_vmem),
            scratch_shapes=scratch,
            compiler_params=pltpu.CompilerParams(
                collective_id=0, has_side_effects=True, vmem_limit_bytes=60 * 1024 * 1024
            ),
        )(block_input, cotangent, matrix, vectors, norm_params, running, resets, lengths.reshape(1, 4))
        out, grad, *rest = pl.pallas_call(
            functools.partial(finish, len(shapes)),
            out_shape=shapes,
            in_specs=[any_space] * len(shapes),
            out_specs=(any_space,) * len(shapes),
            scratch_shapes=[vmem(shape.shape) for shape in shapes] + [dma(2, len(shapes))],
        )(*results)
        return (out[None, None], grad[None, None], *rest)

    return jax.shard_map(
        shards,
        mesh=mesh,
        in_specs=(
            P(None, "dp", None, None),
            P(None, "dp", None, None),
            P("section", None, None),
            P("section", None),
            P(),
            P(),
            P(None, "dp", None),
            P(None, "dp"),
        ),
        out_specs=(
            P("section", "dp", None, None),
            P("section", "dp", None, None),
            P("section", None, None),
            P("section", None),
            P("section", None),
            P("section", None),
        ),
        check_vma=False,
    )
```

profile of v0, /device:TPU:0, one launch (start us, length us, event | category | flops | bytes accessed | tf_op | source)
XLA Modules:
  0.0 139.0 jit_solution(10267516248316218865)
XLA Ops:
  0.6 134.8 %shard_map.127 = (f32[256,512]{1,0:T(8,128)}, f32[256,512]{1,0:T(8,128)}, f32[1,512,1024]{2,1,0:T(8,128)}, f32[2,512]{1,0:T(2,128)}, f32[1,512]{1,0:T(1,128)}, /*index=5*/f32[1,512]{1,0:T(1,128)}) custom-call(f32[4,1,256,512]{3,2,1,0:T(8,128)} %refs_0_.1, f32[4,1,256,512]{3,2,1,0:T(8,128)} %refs_1_.1, f32[1,512,1024]{2,1,0:T(8,128)} %refs_2_.1, ...), custom_call_target="tpu_custom_call" | custom-call | tf_op jit(solution)/shard_map/pallas_call | solution.py:1091
  135.5 3.4 %shard_map.128 = (f32[256,512]{1,0:T(8,128)}, f32[256,512]{1,0:T(8,128)}, f32[1,512,1024]{2,1,0:T(8,128)}, f32[2,512]{1,0:T(2,128)}, f32[1,512]{1,0:T(1,128)}, /*index=5*/f32[1,512]{1,0:T(1,128)}) custom-call(f32[256,512]{1,0:T(8,128)} %get-tuple-element.18.refs_0_, f32[256,512]{1,0:T(8,128)} %get-tuple-element.19.refs_1_, ...), custom_call_target="tpu_custom_call" | custom-call | tf_op jit(solution)/shard_map/pallas_call | solution.py:1101
where the time goes:
time: 139 us
  Pallas kernels  138 us (99%)
    pallas_call x1, Pallas kernels, shards(): pl.pallas_call(functools.partial(kernel, n, T, D), out_shape=shapes, in_s...  135 us
    pallas_call x1, Pallas kernels, shards(): pl.pallas_call(functools.partial(finish, len(shapes)), out_shape=shapes,...  3.36 us

commit v1 on v0

--- a/solution.py
+++ b/solution.py
@@ -19,7 +19,6 @@
 SEGMENTS = (
     ("glu1", 1.8), ("c1", 0.9), ("b1", 0.9), ("stream1", 1.5), ("gate0", 0.8), ("glu0", 1.8),
     ("mixed0", 2.0), ("states0", 0.6), ("c0", 0.9), ("scan0", 2.0), ("b0", 0.9), ("normed0", 1.5),
-    ("stream0", 2.5),
 )
 MAKES = {
     "glu1": (1, 1, (0, 1, 2, 3)), "c1": (1, 0, (0, 1)), "b1": (1, 0, (2, 3)),
@@ -27,24 +26,33 @@
 }
 
 
+METHODS = {(0, 0): "dddd", (0, 1): "xxxx", (1, 0): "xxxx", (1, 1): "dddd"}
+
+
 def far_first(layer, core, j):
-    return layer != core
-
-
-def turned(layer, core, j):
-    return 0
+    return METHODS[layer, core][j] == "x"
+
+
+def stages(k):
+    found, bit = [(0, 2)], 1
+    while bit < k:
+        bits = min(2, k - bit)
+        found.append((bit, 1 << bits))
+        bit += bits
+    return found
 
 
 def step_kinds(layer, core, j, k, owner):
-    halving = [("halve", stage) for stage in range(k)]
-    doubling = [("double", stage) for stage in reversed(range(k))]
+    count = len(stages(k))
+    halving = [("halve", stage) for stage in range(count)]
+    doubling = [("double", stage) for stage in reversed(range(count))]
     if far_first(layer, core, j):
         return [("core", 0)] + ([("far", 0)] + halving + doubling if owner else [])
     return [("core", 0)] + halving + ([("far", k)] + doubling if owner else [])
 
 
 def planned(k):
-    chunk, hop, work = 5.2, 1.5, 0.2
+    chunk, far_chunk, core_chunk, hop, work, slow = 4.9, 5.0, 0.85, 1.0, 0.2, 1.0
     roles = [(x, core) for x in range(2) for core in range(2)]
     links = {}
     ready = {role: {} for role in roles}
@@ -66,14 +74,16 @@
         x, core = role
         if kind == "far":
             if x != layer:
-                early[(1 - x, core), layer, j] = send(at, [("x", x)], chunk / (1 << stage))
+                early[(1 - x, core), layer, j] = send(at, [("x", x)], far_chunk / (1 << stage))
             return
-        bit = (stage + turned(layer, core, j)) % k
-        lasts = chunk / (2 << stage)
-        names = [(x, "z"), (x, "middle"), (x, "middle")] if bit == 2 and k == 3 else [(x, "z" if bit == 1 else bit)]
-        for name in names[2:]:
-            links[name] = links.get(name, 0.0) + lasts
-        ready[role][layer, j] = (kinds(role, layer, j).index((kind, stage)), send(at, names[:2], lasts))
+        share = 1.0
+        for _, radix in stages(k)[:stage]:
+            share /= radix
+        radix = stages(k)[stage][1]
+        end = send(at, [(x, stage)], chunk * share * (radix - 1) / radix)
+        if radix == 4:
+            end = max(end, send(at, [(x, stage, "middle")], chunk * share)) + 1.0
+        ready[role][layer, j] = (kinds(role, layer, j).index((kind, stage)), end)
 
     def run(role, layer, j):
         step, at = ready[role].pop((layer, j))
@@ -100,7 +110,7 @@
         for role in roles:
             working = place[role] < len(SEGMENTS)
             known = [
-                (at + (3.0 if working and step > 0 else 0.0), key)
+                (at + (1.0 if working and step > 0 else 0.0), key)
                 for key, (step, at) in ready[role].items() if at is not None
             ]
             due = [(-key[0], at, key) for at, key in known if at <= now[role]]
@@ -122,13 +132,46 @@
         if name in MAKES and MAKES[name][1] != role[1]:
             layer, core, chunks = MAKES[name]
             for j in chunks:
-                ready[role[0], core][layer, j] = (0, send(now[role], [("core", role)], chunk / 6))
+                ready[role[0], core][layer, j] = (0, send(now[role], [("core", role)], core_chunk))
     return order, now
 
 
 def split(value):
     high = value.astype(bf16)
     return high, (value - high.astype(f32)).astype(bf16)
+
+
+def inverted(value):
+    rough = pl.reciprocal(value, approx=True)
+    rough = rough * (2.0 - value * rough)
+    return rough * (2.0 - value * rough)
+
+
+ERF_TOP = (
+    -2.72614225801306e-10, 2.77068142495902e-08, -2.10102402082508e-06, -5.69250639462346e-05,
+    -7.34990630326855e-04, -2.95459980854025e-03, -1.60960333262415e-02,
+)
+ERF_BOTTOM = (
+    -1.45660718464996e-05, -2.13374055278905e-04, -1.68282697438203e-03, -7.37332916720468e-03,
+    -1.42647390514189e-02,
+)
+
+
+def erf(value):
+    value = jnp.clip(value, -3.832506856900711, 3.832506856900711)
+    square = value * value
+    top = bottom = None
+    for factor in ERF_TOP:
+        top = factor if top is None else top * square + factor
+    for factor in ERF_BOTTOM:
+        bottom = factor if bottom is None else bottom * square + factor
+    return value * top * -inverted(-bottom)
+
+
+def sigmoid(value):
+    small = jnp.exp(-jnp.abs(value))
+    share = inverted(1.0 + small)
+    return jnp.where(value >= 0.0, share, small * share)
 
 
 def fold(value):
@@ -226,6 +269,8 @@
 
     count = jnp.full((1, D), length.astype(f32), f32)
 
+    short = n <= 8
+
     def send_round(index, tiles):
         def go(j, carry):
             remote(
@@ -234,17 +279,21 @@
             ).start()
             return carry
 
-        lax.fori_loop(1, n, go, 0)
-
-    def wait_round(index, tiles):
+        lax.fori_loop(1, n, go, 0, unroll=short)
+
+    def wait_round(index, tiles, sent=False):
         def go(j, carry):
-            remote(
+            copy = remote(
                 smsg.at[index, pl.ds(0, tiles)], sbuf.at[index, d, pl.ds(0, tiles)],
                 sts.at[index, j], stq.at[index, j], (lax.rem(d + j, n), s),
-            ).wait()
+            )
+            if sent:
+                copy.wait_send()
+            else:
+                copy.wait_recv()
             return carry
 
-        lax.fori_loop(1, n, go, 0)
+        lax.fori_loop(1, n, go, 0, unroll=short)
 
     def pack(index, tile, first, second):
         for j in range(lanes):
@@ -256,11 +305,13 @@
         row = [tmp8[j : j + 1, :] for j in range(2 * lanes)]
         return jnp.concatenate(row[:lanes], axis=1), jnp.concatenate(row[lanes:], axis=1)
 
-    def local_moments(layer):
+    def local_moments(layer, total=None):
         def first(rows, total):
             return total + fold(usable_at(rows) * xs[layer, rows, :])
 
-        total = jnp.sum(rows_loop(first, jnp.zeros((8, D), f32)), axis=0, keepdims=True)
+        if total is None:
+            total = rows_loop(first, jnp.zeros((8, D), f32))
+        total = jnp.sum(total, axis=0, keepdims=True)
         mean = total / jnp.maximum(count, 1.0)
 
         def second(rows, squares):
@@ -281,7 +332,7 @@
             return carry[0] + sbuf[layer, j, 0], carry[1] + sbuf[0, j, 1]
 
         zero = jnp.zeros((8, 128), f32)
-        total, counted = lax.fori_loop(0, n, add, (zero, zero))
+        total, counted = lax.fori_loop(0, n, add, (zero, zero), unroll=short)
         tmp8[...] = total / counted
         center = tmp8[0:lanes, :]
 
@@ -290,7 +341,7 @@
             apart = sbuf[layer, j, 0][0:lanes, :] / jnp.maximum(there, 1.0) - center
             return carry + there * apart * apart
 
-        apart = lax.fori_loop(0, n, between, jnp.zeros((lanes, 128), f32))
+        apart = lax.fori_loop(0, n, between, jnp.zeros((lanes, 128), f32), unroll=short)
         center_row, spread_row = unpack(total / counted)
         tmp8[0:lanes, :] = apart / counted[0:lanes, :]
         apart_row = jnp.concatenate([tmp8[j : j + 1, :] for j in range(lanes)], axis=1)
@@ -349,19 +400,20 @@
         def _():
             convert(q, p)
 
-    events = []
+    events = ([], [])
     for i in range(2 * CHUNKS + 2):
-        if i < 2 * CHUNKS:
-            events.append((arrive, i))
-        if 0 <= i - 1 < 2 * CHUNKS:
-            events.append((arrive_pair, i - 1))
-        if 0 <= i - 2 < 2 * CHUNKS:
-            events.append((arrive_sibling, i - 2))
+        for plane in range(2):
+            if i < 2 * CHUNKS:
+                events[plane].append((arrive, i))
+            if 0 <= i - 1 < 2 * CHUNKS:
+                events[plane].append((arrive_pair, i - 1))
+            if 0 <= i - 2 < 2 * CHUNKS:
+                events[plane].append((arrive_sibling, i - 2))
     passed = [0, 0]
 
     def until(plane, what):
-        stop = events.index(what) + 1 if what is not None else len(events)
-        todo = events[passed[plane] : stop]
+        stop = events[plane].index(what) + 1
+        todo = events[plane][passed[plane] : stop]
         passed[plane] = max(passed[plane], stop)
         if todo:
 
@@ -373,26 +425,36 @@
     def vector_copy(j):
         return remote(V.at[s], V.at[s], vs.at[j], vr.at[j], (d, lax.rem(s + j, 4)))
 
-    def bit_value(task, stage):
-        return 1 << ((stage + turned(*task)) % k)
-
-    def my_bit(task, stage):
-        return (d // bit_value(task, stage)) % 2
-
-    def partner(task, stage):
-        return (d + bit_value(task, stage) * (1 - 2 * my_bit(task, stage)), s)
-
-    def segment(task, stage, mine):
+    levels = stages(k)
+    sizes = [D]
+    for _, radix in levels:
+        sizes.append(sizes[-1] // radix)
+    starts = [0]
+    for (_, radix), size in zip(levels, sizes[1:]):
+        starts.append(starts[-1] + (radix - 1) * size)
+
+    def digit(stage):
+        bit, radix = levels[stage]
+        return (d // (1 << bit)) % radix
+
+    def peer(stage, turn):
+        bit, radix = levels[stage]
+        place = (digit(stage) + turn) % radix
+        return place, (d + (place - digit(stage)) * (1 << bit), s)
+
+    def segment(stage, place=None):
         start = 0
         for earlier in range(stage):
-            start = start + my_bit(task, earlier) * (D >> (earlier + 1))
-        bit = my_bit(task, stage) if mine else 1 - my_bit(task, stage)
-        size = D >> (stage + 1)
-        return pl.ds(pl.multiple_of(start + bit * size, size), size)
-
-    def landing(stage):
-        size = D >> (stage + 1) if stage < k else D >> k
-        return pl.ds(D - (D >> stage), size)
+            start = start + digit(earlier) * sizes[earlier + 1]
+        start = start + (digit(stage) if place is None else place) * sizes[stage + 1]
+        return pl.ds(pl.multiple_of(start, sizes[stage + 1]), sizes[stage + 1])
+
+    def landing(stage, turn=1):
+        if stage == len(levels):
+            return pl.ds(starts[stage], sizes[stage])
+        return pl.ds(starts[stage] + (turn - 1) * sizes[stage + 1], sizes[stage + 1])
+
+    last = len(levels) - 1
 
     def column(core, j):
         return j if core == 1 else (j + 2) % CHUNKS
@@ -407,38 +469,47 @@
         layer, core, j = task
         return G.at[2 * layer + core, column(core, j)]
 
-    def halving_copy(task, stage):
+    def halving_copies(task, stage):
         layer, core, j = task
-        return remote(
-            mine_of(task).at[segment(task, stage, False)], RB.at[layer, j, landing(stage)],
-            rss.at[layer, j, stage], rsr.at[layer, j, stage], partner(task, stage),
-        )
+        copies = []
+        for turn in range(1, levels[stage][1]):
+            place, device = peer(stage, turn)
+            copies.append(remote(
+                mine_of(task).at[segment(stage, place)], RB.at[layer, j, landing(stage, turn)],
+                rss.at[layer, j, 3 * stage + turn], rsr.at[layer, j, 3 * stage + turn], device,
+            ))
+        return copies
 
     def far_copy(task):
         layer, core, j = task
         if far_first(*task):
             source, target = mine_of(task), XB.at[j]
         else:
-            source, target = mine_of(task).at[segment(task, k - 1, True)], RB.at[layer, j, landing(k)]
-        return remote(source, target, rss.at[layer, j, k], rsr.at[layer, j, k], far)
-
-    def doubling_copy(task, stage):
+            source, target = mine_of(task).at[segment(last)], RB.at[layer, j, landing(last + 1)]
+        return remote(source, target, rss.at[layer, j, 0], rsr.at[layer, j, 0], far)
+
+    def doubling_copies(task, stage):
         layer, core, j = task
-        ref = R.at[column(core, j), segment(task, stage, True)]
-        return remote(ref, ref, ags.at[j, stage], agr.at[j, stage], partner(task, stage))
+        ref = R.at[column(core, j), segment(stage)]
+        return [
+            remote(
+                ref, ref, ags.at[j, 3 * stage + turn], agr.at[j, 3 * stage + turn], peer(stage, turn)[1]
+            )
+            for turn in range(1, levels[stage][1])
+        ]
 
     def result_copy(j):
         return pltpu.make_async_copy(R.at[j], matrix_out.at[0, :, pl.ds(j * W2, W2)], lsem.at[6 + j])
 
-    def add_rows(target, start, mine, mine_start, source, source_start, size):
+    def add_rows(target, start, mine, sources, size):
         step = min(size, 32)
 
         def body(i, carry):
-            a, b, e = (
-                pl.ds(pl.multiple_of(first + i * step, 8), step)
-                for first in (start, mine_start, source_start)
-            )
-            target[a, :] = mine[b, :] + source[e, :]
+            rows = pl.ds(pl.multiple_of(start + i * step, 8), step)
+            total = mine[rows, :]
+            for source, first in sources:
+                total = total + source[pl.ds(pl.multiple_of(first + i * step, 8), step), :]
+            target[rows, :] = total
             return carry
 
         lax.fori_loop(0, size // step, body, 0, unroll=min(2, size // step))
@@ -453,29 +524,34 @@
         target = total if after is not None and after[0] == "double" else mine
         if kind == "core":
             sibling_copy(core, layer, j).wait_recv()
-            add_rows(target, 0, mine, 0, SB.at[layer, j], 0, D)
+            add_rows(target, 0, mine, [(SB.at[layer, j], 0)], D)
         elif kind == "far":
             far_copy(task).wait_recv()
             if far_first(*task):
-                add_rows(target, 0, mine, 0, XB.at[j], 0, D)
+                add_rows(target, 0, mine, [(XB.at[j], 0)], D)
             else:
-                kept = segment(task, k - 1, True)
-                add_rows(target, kept.start, mine, kept.start, RB.at[layer, j], landing(k).start, kept.size)
+                kept, source = segment(last), (RB.at[layer, j], landing(last + 1).start)
+                add_rows(target, kept.start, mine, [source], kept.size)
         elif kind == "halve":
-            halving_copy(task, stage).wait()
-            kept = segment(task, stage, True)
-            add_rows(target, kept.start, mine, kept.start, RB.at[layer, j], landing(stage).start, kept.size)
+            for copy in halving_copies(task, stage):
+                copy.wait()
+            kept = segment(stage)
+            sources = [
+                (RB.at[layer, j], landing(stage, turn).start) for turn in range(1, levels[stage][1])
+            ]
+            add_rows(target, kept.start, mine, sources, kept.size)
         else:
-            doubling_copy(task, stage).wait()
+            for copy in doubling_copies(task, stage):
+                copy.wait()
         if after is None:
             result_copy(column(core, j)).start()
         elif after[0] == "far":
             if plane != layer:
                 far_copy(task).start()
-        elif after[0] == "halve":
-            halving_copy(task, after[1]).start()
         else:
-            doubling_copy(task, after[1]).start()
+            copies = halving_copies if after[0] == "halve" else doubling_copies
+            for copy in copies(task, after[1]):
+                copy.start()
 
     plans = planned(k)[0]
 
@@ -745,7 +821,7 @@
 
         def activate(rows, carry):
             mixed = mx[rows, :] + skip * nf[layer, rows, :]
-            phi = 0.5 * (1.0 + lax.erf(mixed * 0.7071067811865476))
+            phi = 0.5 * (1.0 + erf(mixed * 0.7071067811865476))
             dge[layer, rows, :] = phi + mixed * (0.3989422804014327 * jnp.exp(-0.5 * mixed * mixed))
             active = mixed * phi
             af[rows, :] = active
@@ -767,12 +843,15 @@
 
         def gate(rows, carry):
             value = jv[layer, rows, :] + value_bias
-            sig = 1.0 / (1.0 + jnp.exp(-(js[layer, rows, :] + gate_bias)))
+            sig = sigmoid(js[layer, rows, :] + gate_bias)
             jv[layer, rows, :] = value
             js[layer, rows, :] = sig
-            target[rows, :] = xs[layer, rows, :] + usable_at(rows) * (value * sig)
-
-        rows_loop(gate)
+            usable = usable_at(rows)
+            result = xs[layer, rows, :] + usable * (value * sig)
+            target[rows, :] = result
+            return carry + fold(usable * result)
+
+        return rows_loop(gate, jnp.zeros((8, D), f32))
 
     def gate_back(layer):
         def body(rows, carry):
@@ -819,12 +898,12 @@
                     high_ref[layer, t, u : u + 128] = high
                     low_ref[layer, t, u : u + 128] = low
 
-    def weight_back(q, chunks, left, right, columns):
+    def weight_back(q, chunks, left, right, columns, first=0):
         def keep(column, rows, value):
             G[q, chunks[column], rows, :] = value
 
         multiply(
-            left, lambda part, step, column: right[part][tile(step), tile(column)], T, columns, keep
+            left, lambda part, step, column: right[part][tile(step), tile(first + column)], T, columns, keep
         )
 
     def hand_over(core, layer, chunks):
@@ -834,10 +913,12 @@
                 sibling_copy(core, layer, j).start()
 
     def glu_back(layer):
-        weight_back(
-            2 * layer + 1, range(CHUNKS), (ath.at[layer], atl.at[layer]), (djh, djl), CHUNKS
-        )
-        hand_over(0, layer, range(CHUNKS))
+        for pair in range(2):
+            chunks = (2 * pair, 2 * pair + 1)
+            weight_back(
+                2 * layer + 1, chunks, (ath.at[layer], atl.at[layer]), (djh, djl), 2, 2 * pair
+            )
+            hand_over(0, layer, chunks)
 
     def c_back(layer):
         weight_back(2 * layer, (2, 3), (sth.at[layer], stl.at[layer]), (dmh, dml), 2)
@@ -869,7 +950,8 @@
         wait_round(2 + layer, 1)
         sbuf[2 + layer, d, 0] = smsg[2 + layer, 0]
         total = lax.fori_loop(
-            0, n, lambda j, carry: carry + sbuf[2 + layer, j, 0], jnp.zeros((8, 128), f32)
+            0, n, lambda j, carry: carry + sbuf[2 + layer, j, 0], jnp.zeros((8, 128), f32),
+            unroll=short,
         )
         gain_total, offset_total = unpack(total)
         emsg[2 * layer, 2:3, :] = gain_total
@@ -891,7 +973,7 @@
     wait_round(0, 2)
     for layer in range(2):
         if layer == 1:
-            local_moments(1)
+            local_moments(1, total)
             send_round(1, 1)
             turn(0)
             until(0, (arrive_sibling, 1))
@@ -902,7 +984,7 @@
         inverse = lax.rsqrt(spread + epsilon)
         rowbuf[2 * layer : 2 * layer + 1, :] = center
         rowbuf[2 * layer + 1 : 2 * layer + 2, :] = inverse
-        forward(layer, center, inverse)
+        total = forward(layer, center, inverse)
 
     store_out = pltpu.make_async_copy(xs.at[2], out_ref, lsem.at[10])
     store_grad = pltpu.make_async_copy(gx, grad_ref, lsem.at[11])
@@ -934,12 +1016,9 @@
         ("scan0", lambda: backward_scan(0)),
         ("b0", lambda: b_back(0)),
         ("normed0", lambda: normed_back(0, center, inverse)),
-        ("stream0", lambda: stream_back(0, center, inverse, counted)),
     ):
         steps_before(name)
         work()
-
-    store_grad.start()
 
     def vector_round(j):
         return remote(vmsg, vbuf.at[d], sts.at[4, j], stq.at[4, j], (lax.rem(d + j, n), s))
@@ -959,12 +1038,15 @@
     def rest(part):
         def of(role):
             steps = plans[role]["rest"]
-            cut = len(steps) // 3
-            return steps[:cut] if part == 0 else steps[cut:]
+            cuts = (0, len(steps) // 4, len(steps) // 2, len(steps))
+            return steps[cuts[part] : cuts[part + 1]]
 
         return of
 
     by_role(rest(0))
+    stream_back(0, center, inverse, counted)
+    store_grad.start()
+    by_role(rest(1))
 
     def arrived(j, carry):
         vector_round(j).wait()
@@ -977,7 +1059,7 @@
         emsg[q, 0:2, :] = total[2 * q : 2 * q + 2, :]
     for j in range(1, 4):
         owner_copy(j).start()
-    by_role(rest(1))
+    by_role(rest(2))
 
     for j in range(1, 4):
         owner_copy(j).wait()
@@ -995,6 +1077,8 @@
     norm_out[...] = norm_total
     running_out[...] = current
 
+    for index in range(4):
+        wait_round(index, 2 if index == 0 else 1, sent=True)
     for p in range(CHUNKS):
         own_copy(p).wait_send()
     for i in range(2 * CHUNKS):
@@ -1022,16 +1106,23 @@
 
 def finish(count, *refs):
     given, results, held, sems = refs[:count], refs[count : 2 * count], refs[2 * count : 3 * count], refs[-1]
-    steps = [
-        [pltpu.make_async_copy(a, b, sems.at[way, i]) for i, (a, b) in enumerate(zip(*pair))]
-        for way, pair in enumerate(((given, held), (held, results)))
-    ]
-    for copy in steps[0]:
+    triples = []
+    for triple in zip(given, held, results):
+        rows = triple[0].shape[-2]
+        if rows % 4 == 0 and rows >= 256:
+            for part in range(4):
+                cut = pl.ds(part * (rows // 4), rows // 4)
+                triples.append([ref.at[0, cut] if len(ref.shape) == 3 else ref.at[cut] for ref in triple])
+        else:
+            triples.append(list(triple))
+    first = [pltpu.make_async_copy(a, b, sems.at[0, i]) for i, (a, b, _) in enumerate(triples)]
+    second = [pltpu.make_async_copy(b, e, sems.at[1, i]) for i, (_, b, e) in enumerate(triples)]
+    for copy in first:
         copy.start()
-    for first, second in zip(*steps):
-        first.wait()
-        second.start()
-    for copy in steps[1]:
+    for copy, after in zip(first, second):
+        copy.wait()
+        after.start()
+    for copy in second:
         copy.wait()
 
 
@@ -1074,7 +1165,7 @@
             vmem((2, 8, S)), vmem((2, 3, 8, S)),
             vmem((T, D)),
             dma(12), dma(5, 8), dma(5, 8), dma(2, 4), dma(2, 4),
-            dma(2, 4, k + 1), dma(2, 4, k + 1), dma(4, k), dma(4, k),
+            dma(2, 4, 3 * k + 1), dma(2, 4, 3 * k + 1), dma(4, 3 * k + 1), dma(4, 3 * k + 1),
             dma(5, n), dma(5, n), dma(4), dma(4), dma(4), dma(4),
         ]
         any_space = pl.BlockSpec(memory_space=pl.ANY)
@@ -1103,7 +1194,7 @@
             out_shape=shapes,
             in_specs=[any_space] * len(shapes),
             out_specs=(any_space,) * len(shapes),
-            scratch_shapes=[vmem(shape.shape) for shape in shapes] + [dma(2, len(shapes))],
+            scratch_shapes=[vmem(shape.shape) for shape in shapes] + [dma(2, 4 * len(shapes))],
         )(*results)
         return (out[None, None], grad[None, None], *rest)
 

time: 139 us -> 139 us (level)
  no operation moved by 1% of the time
where the time goes in v1:
time: 139 us
  Pallas kernels  138 us (99%)
    pallas_call x1, Pallas kernels, shards(): pl.pallas_call(functools.partial(kernel, n, T, D), out_shape=shapes, in_s...  135 us
    pallas_call x1, Pallas kernels, shards(): pl.pallas_call(functools.partial(finish, len(shapes)), out_shape=shapes,...  3.47 us

profile of v1, /device:TPU:0, one launch (start us, length us, event | category | flops | bytes accessed | tf_op | source)
XLA Modules:
  0.0 139.1 jit_solution(3730477434781253389)
XLA Ops:
  0.6 134.8 %shard_map.127 = (f32[256,512]{1,0:T(8,128)}, f32[256,512]{1,0:T(8,128)}, f32[1,512,1024]{2,1,0:T(8,128)}, f32[2,512]{1,0:T(2,128)}, f32[1,512]{1,0:T(1,128)}, /*index=5*/f32[1,512]{1,0:T(1,128)}) custom-call(f32[4,1,256,512]{3,2,1,0:T(8,128)} %refs_0_.1, f32[4,1,256,512]{3,2,1,0:T(8,128)} %refs_1_.1, f32[1,512,1024]{2,1,0:T(8,128)} %refs_2_.1, ...), custom_call_target="tpu_custom_call" | custom-call | tf_op jit(solution)/shard_map/pallas_call | solution.py:1182
  135.4 3.5 %shard_map.128 = (f32[256,512]{1,0:T(8,128)}, f32[256,512]{1,0:T(8,128)}, f32[1,512,1024]{2,1,0:T(8,128)}, f32[2,512]{1,0:T(2,128)}, f32[1,512]{1,0:T(1,128)}, /*index=5*/f32[1,512]{1,0:T(1,128)}) custom-call(f32[256,512]{1,0:T(8,128)} %get-tuple-element.18.refs_0_, f32[256,512]{1,0:T(8,128)} %get-tuple-element.19.refs_1_, ...), custom_call_target="tpu_custom_call" | custom-call | tf_op jit(solution)/shard_map/pallas_call | solution.py:1192
